TPU v7x, 256 devices: a whole 4x4x8 slice. The times are simulated.
256 devices in a mesh: wide: 32 (over x, z), narrow: 8 (over y, core).
Axes of the slice: x: 4, y: 4, z: 8, core: 2. Of those that a mesh axis runs over, the one named last changes fastest.
Arguments:
- ensemble: bfloat16 [1024, 262144], P('narrow', 'wide'), may hold values from -6 to 6
- owner: int32 [2048], P('wide'), may hold values from 0 to 255, as said below
- inflation: float32 [256], replicated, may hold values from 1 to 2
- obs_block: int32 [512], P('wide'), may hold values from 0 to 63
- obs_value: float32 [65536], P('wide'), may hold values from -12 to 12
- obs_std: float32 [65536], P('wide'), may hold values from 1 to 300
Outputs:
- analysis: bfloat16 [1024, 262144], P('narrow', 'wide')
Inputs may be any that keep to these rules, and one draw needn't show every extreme that they name: `obs_block`: indexes one of the 64 state blocks held by the same index of wide as the observations. `owner`: a state block held by index w of wide belongs to one of the compartments w * 8 to w * 8 + 7.
All inputs are finite; a program needn't handle non-finite values.
Results may differ from a plain program's by a relative error of at most 0.0069.
Values may be sent and summed in bfloat16 or wider, within the bound.
A program may use at most 64 MiB of HBM per device.

v0:
```python
import math

import jax
import jax.numpy as jnp
from jax import lax
from jax.sharding import PartitionSpec as P

CLASSES = 128
ITERS = 4


HIGH = lax.Precision.HIGHEST


def row_identity(row_count, members, first_row):
    row_ids = lax.broadcasted_iota(jnp.int32, (row_count, members), 0) + first_row
    col_ids = lax.broadcasted_iota(jnp.int32, (row_count, members), 1)
    return (row_ids == col_ids).astype(jnp.float32)


def on_device(ensemble, owner, inflation, obs_block, obs_value, obs_std):
    local_members, local_states = ensemble.shape
    members = local_members * lax.axis_size("narrow")
    block_count = local_states // CLASSES
    obs_local = obs_value.shape[0]
    scale_root = math.sqrt(members - 1)
    column_sum = jnp.sum(ensemble, axis=0, dtype=jnp.float32)
    state_mean = lax.psum(column_sum, "narrow") / members
    compartments = lax.broadcasted_iota(jnp.int32, (block_count, inflation.shape[0]), 1)
    block_factor = jnp.sum(
        jnp.where(owner[:, None] == compartments, inflation[None, :], 0.0), axis=1
    )
    row_factor = jnp.repeat(block_factor, CLASSES)
    anomaly = (row_factor * (ensemble.astype(jnp.float32) - state_mean)).astype(jnp.bfloat16)
    observed = jnp.take(anomaly.reshape(local_members, block_count, CLASSES), obs_block, axis=1)
    observed = observed.reshape(local_members, obs_local)
    observed_mean = jnp.take(state_mean.reshape(block_count, CLASSES), obs_block, axis=0).reshape(
        obs_local
    )
    scaled = (observed.astype(jnp.float32) / (obs_std * scale_root)).astype(jnp.bfloat16)
    innovation = (obs_value - observed_mean) / obs_std
    spread = lax.all_to_all(scaled, "narrow", split_axis=1, concat_axis=0, tiled=True)
    obs_share = spread.shape[1]
    narrow_index = lax.axis_index("narrow")
    innovation_share = lax.dynamic_slice_in_dim(innovation, narrow_index * obs_share, obs_share)
    projected_part = jnp.dot(spread.astype(jnp.float32), innovation_share, precision=HIGH)
    row_count = members // lax.axis_size("wide")
    first_row = lax.axis_index("wide") * row_count
    identity_rows = row_identity(row_count, members, first_row)
    contract = (((1,), (1,)), ((), ()))
    gram_part = lax.dot_general(spread, spread, contract, preferred_element_type=jnp.float32)
    gram_sum, projected = lax.psum((gram_part, projected_part), ("wide", "narrow"))
    gram_matrix = gram_sum + jnp.eye(members, dtype=jnp.float32)
    frob_norm = jnp.sqrt(jnp.sum(gram_matrix * gram_matrix))
    gram_rows = lax.dynamic_slice_in_dim(gram_matrix, first_row, row_count, 0)
    unit_rows = gram_rows / frob_norm
    iterate = 1.5 * identity_rows - 0.5 * unit_rows
    for turn_index in range(ITERS - 1):
        iterate_all = lax.all_gather(iterate, "wide", axis=0, tiled=True)
        product_one = jnp.dot(unit_rows, iterate_all, precision=HIGH)
        product_two = jnp.dot(product_one, iterate_all, precision=HIGH)
        iterate = 1.5 * iterate - 0.5 * jnp.dot(product_two, iterate_all, precision=HIGH)
    root_rows = iterate / jnp.sqrt(frob_norm)
    midway_rows = jnp.dot(root_rows, projected, precision=HIGH)
    midway = lax.all_gather(midway_rows, "wide", axis=0, tiled=True)
    mean_shift = jnp.dot(root_rows, midway, precision=HIGH) / scale_root
    transform_part = (root_rows + mean_shift[:, None]).astype(jnp.bfloat16)
    transform = lax.all_gather(transform_part, "wide", axis=0, tiled=True)
    state_share = lax.all_to_all(anomaly, "narrow", split_axis=1, concat_axis=0, tiled=True)
    row_share = state_share.shape[1]
    mean_share = lax.dynamic_slice_in_dim(state_mean, narrow_index * row_share, row_share)
    update = lax.dot_general(
        transform, state_share, (((0,), (0,)), ((), ())), preferred_element_type=jnp.float32
    )
    analysis_share = (mean_share[None, :] + update).astype(jnp.bfloat16)
    return lax.all_to_all(analysis_share, "narrow", split_axis=0, concat_axis=1, tiled=True)


def solution(mesh):
    return jax.shard_map(
        on_device,
        mesh=mesh,
        in_specs=(P("narrow", "wide"), P("wide"), P(), P("wide"), P("wide"), P("wide")),
        out_specs=P("narrow", "wide"),
        check_vma=False,
    )
```

profile of v0, /device:TPU:1, one launch (start us, length us, event | category | flops | bytes accessed | tf_op | source)
XLA Modules:
  0.0 804.0 jit_solution(8070181823294726320)
XLA Ops:
  6.5 0.7 compare_and_fusion
  7.2 0.7 compare_select_fusion
  7.9 0.1 copy.19
  8.1 0.7 broadcast_multiply_fusion.1
  8.8 0.9 select_reduce_fusion
  9.8 3.2 copy.18
  13.0 0.6 convert_reduce_fusion
  13.6 23.8 %psum.21 = f32[8192]{0:T(1024)S(1)} all-reduce(f32[8192]{0:T(1024)S(1)} %convert_reduce_fusion), channel_id=1, replica_groups=mesh['wide'=32,'narrow'=8] {'narrow'}, use_global_device_ids=true, to_apply=%region_1.0 | all-reduce | flops 8192 | bytes 65536 | tf_op jit(solution)/shard_map/psum | solution.py:28
  37.5 5.5 fusion.1
  43.0 3.2 copy.20
  46.2 0.6 gather_fusion
  46.9 0.3 copy.21
  47.2 0.7 divide_convert_fusion
  47.9 15.3 %all_to_all.54 = bf16[128,8,256]{0,2,1:T(8,128)(2,1)S(1)} all-to-all(bf16[128,8,256]{0,2,1:T(8,128)(2,1)S(1)} %divide_convert_fusion), channel_id=1, replica_groups=mesh['wide'=32,'narrow'=8] {'narrow'}, dimensions={1} | all-to-all | bytes 1048576 | tf_op jit(solution)/shard_map/all_to_all | solution.py:42
  63.2 0.2 copy.22
  63.4 2.7 fusion.11
  66.2 268.4 %all-reduce.3.cloned.1.call-done = f32[1024,1024]{1,0:T(8,128)} async-done(((f32[1024,1024]{1,0:T(8,128)}), f32[1024,1024]{1,0:T(8,128)}) %all-reduce.3.cloned.1.call-update) | async-done | bytes 4194320 | tf_op jit(solution)/shard_map/psum | solution.py:52
  334.6 5.9 convert_add_fusion
  341.2 1.6 multiply_subtract_fusion
  342.9 79.5 %all-gather.5.cloned.1.call-done = f32[1024,1024]{1,0:T(8,128)} async-done(((f32[32,1024]{1,0:T(8,128)}), f32[1024,1024]{1,0:T(8,128)}) %all-gather.5.cloned.1.call-update) | async-done | bytes 4194320 | tf_op jit(solution)/shard_map/all_gather | solution.py:59
  422.4 4.9 fusion.10
  427.3 2.5 fusion.12
  429.8 3.1 fusion.5
  433.0 0.2 all-gather.9.cloned.1.call-start
  433.2 78.9 %all-gather.7.cloned.1.call-done = f32[1024,1024]{1,0:T(8,128)} async-done(((f32[32,1024]{1,0:T(8,128)}), f32[1024,1024]{1,0:T(8,128)}) %all-gather.7.cloned.1.call-update) | async-done | bytes 4194320 | tf_op jit(solution)/shard_map/all_gather | solution.py:59
  512.1 4.9 fusion.9
  517.0 2.5 fusion.13
  519.5 3.1 fusion.4
  522.8 0.6 gather_fusion.1
  523.3 0.6 dynamic-slice
  524.7 0.8 dynamic-slice_divide_fusion.1
  525.5 0.5 fusion.15
  526.0 78.5 %psum.23 = f32[1024]{0:T(1024)S(1)} all-reduce(f32[1024]{0:T(1024)S(1)} %bitcast.69), channel_id=1, replica_groups=mesh['wide'=32,'narrow'=8] {'wide','narrow'}, use_global_device_ids=true, to_apply=%region_5.6 | all-reduce | flops 1024 | bytes 8192 | tf_op jit(solution)/shard_map/psum | solution.py:52
  604.6 4.9 fusion.8
  609.5 2.5 fusion.14
  612.0 2.5 fusion.3
  614.5 0.2 convolution_bitcast_fusion.1
  614.7 0.2 dynamic-update-slice
  614.9 56.0 %all-reduce = f32[1024]{0:T(1024)S(1)} all-reduce(f32[1024]{0:T(1024)S(1)} %dynamic-update-slice), channel_id=1, replica_groups=mesh['wide'=32,'narrow'=8] {'wide'}, use_global_device_ids=true, to_apply=%add | all-reduce | flops 1024 | bytes 8192
  670.9 0.2 fusion.6
  671.1 0.7 add_convert_fusion.1
  671.8 21.5 %all-to-all-start.1 = ((bf16[128,8,1024]{0,2,1:T(8,128)(2,1)}), bf16[128,8,1024]{0,2,1:T(8,128)(2,1)S(1)}, u32[]{:S(2)}, u32[]{:S(2)}) async-start(bf16[128,8,1024]{0,2,1:T(8,128)(2,1)} %bitcast.16), calls=%async_computation.1 | async-start | bytes 4194304 | tf_op jit(solution)/shard_map/all_to_all | solution.py:69
  693.4 26.3 %all-to-all-done.1 = bf16[128,8,1024]{0,2,1:T(8,128)(2,1)S(1)} async-done(((bf16[128,8,1024]{0,2,1:T(8,128)(2,1)}), bf16[128,8,1024]{0,2,1:T(8,128)(2,1)S(1)}, u32[]{:S(2)}, u32[]{:S(2)}) %all-to-all-start.1) | async-done | bytes 2097184 | tf_op jit(solution)/shard_map/all_to_all | solution.py:69
  719.7 2.6 copy.23
  722.3 33.9 %all-gather.11.cloned.1.call-done = bf16[1024,1024]{1,0:T(8,128)(2,1)} async-done(((bf16[32,1024]{1,0:T(8,128)(2,1)}), bf16[1024,1024]{1,0:T(8,128)(2,1)}) %all-gather.11.cloned.1.call-update) | async-done | bytes 2097168 | tf_op jit(solution)/shard_map/all_gather | solution.py:68
  756.2 4.6 add_convert_fusion
  760.8 35.1 %all_to_all.55 = bf16[8,128,1024]{2,1,0:T(8,128)(2,1)S(1)} all-to-all(bf16[8,128,1024]{2,1,0:T(8,128)(2,1)S(1)} %bitcast.65), channel_id=1, replica_groups=mesh['wide'=32,'narrow'=8] {'narrow'}, dimensions={0} | all-to-all | bytes 4194304 | tf_op jit(solution)/shard_map/all_to_all | solution.py:76
  795.9 1.5 copy.25
  (34 shorter events, 0.6 us)
Async XLA Ops:
  6.5 328.1 %all-reduce.3.cloned.1.call-start = ((), (), s32[]{:S(2)}) async-start(), calls=%async_computation.3 | async-start | bytes 8388608 | tf_op jit(solution)/shard_map/psum | solution.py:52
  66.1 356.3 %all-gather.5.cloned.1.call-start = ((), (), s32[]{:S(2)}) async-start(), calls=%async_computation.4 | async-start | bytes 4325376 | tf_op jit(solution)/shard_map/all_gather | solution.py:59
  342.9 86.9 %copy-start.5 = (f32[32,1024]{1,0:T(8,128)S(1)}, f32[32,1024]{1,0:T(8,128)}, u32[]{:S(2)}) copy-start(f32[32,1024]{1,0:T(8,128)} %multiply_subtract_fusion) | copy-start | bytes 393220
  342.9 169.3 %all-gather.7.cloned.1.call-start = ((), (), s32[]{:S(2)}) async-start(), calls=%async_computation.5 | async-start | bytes 4325376 | tf_op jit(solution)/shard_map/all_gather | solution.py:59
  422.4 4.9 copy-start.1
  433.0 86.6 %copy-start.4 = (f32[32,1024]{1,0:T(8,128)S(1)}, f32[32,1024]{1,0:T(8,128)}, u32[]{:S(2)}) copy-start(f32[32,1024]{1,0:T(8,128)} %fusion.5) | copy-start | bytes 393220
  433.0 171.6 %all-gather.9.cloned.1.call-start = ((), (), s32[]{:S(2)}) async-start(), calls=%async_computation.6 | async-start | bytes 4325376 | tf_op jit(solution)/shard_map/all_gather | solution.py:59
  512.1 4.9 copy-start.2
  517.0 6.3 copy-start.6
  522.7 233.5 %all-gather.11.cloned.1.call-start = ((), (), s32[]{:S(2)}) async-start(), calls=%async_computation.7 | async-start | bytes 2162688 | tf_op jit(solution)/shard_map/all_gather | solution.py:68
  604.5 7.5 copy-start.3
  604.6 4.9 copy-start
  671.8 47.9 %all-to-all-start.1 = ((bf16[128,8,1024]{0,2,1:T(8,128)(2,1)}), bf16[128,8,1024]{0,2,1:T(8,128)(2,1)S(1)}, u32[]{:S(2)}, u32[]{:S(2)}) async-start(bf16[128,8,1024]{0,2,1:T(8,128)(2,1)} %bitcast.16), calls=%async_computation.1 | async-start | bytes 4194304 | tf_op jit(solution)/shard_map/all_to_all | solution.py:69
Sparse Core Ops, SparseCore 0:
  66.2 268.3 all-reduce.2
  343.0 79.3 all-gather.4
  433.1 78.9 all-gather.6
  522.8 79.3 all-gather.8
  671.9 84.2 all-gather.10
where the time goes:
time: 805 us; the launch traced here: 804 us
  waiting for transfers between devices  487 us (60%)
  blocking collectives  209 us (26%)
  matrix products  39 us (5%)
  starting transfers between devices  21.9 us (3%)
  other arithmetic  18.9 us (2%)
  between operations  14.7 us (2%)
  local copies, waits for them, and re-layouts  13.5 us (2%)
    psum x1, waiting for transfers between devices, on_device(): lax.psum((gram_part, projected_part), ('wide', 'narrow'))  268 us
    all_gather x3, waiting for transfers between devices, on_device(): iterate_all = lax.all_gather(iterate, 'wide', axis=0, tiled=True)  158 us
    psum x1, blocking collectives, on_device(): lax.psum((gram_part, projected_part), ('wide', 'narrow'))  78.5 us
    unnamed x1, blocking collectives  56 us
    all_to_all x1, blocking collectives, on_device(): lax.all_to_all(analysis_share, 'narrow', split_axis=0, concat_axis=1, til...  35.1 us
    all_gather x1, waiting for transfers between devices, on_device(): transform = lax.all_gather(transform_part, 'wide', axis=0, tiled=True)  33.9 us
    all_to_all x1, waiting for transfers between devices, on_device(): lax.all_to_all(anomaly, 'narrow', split_axis=1, concat_axis=0, tiled=True)  26.3 us
    psum x1, blocking collectives, on_device(): state_mean = lax.psum(column_sum, 'narrow') / members  23.8 us
  transfers between devices with their start and end apart: 6, of which 5 were waited for; matrix products, arithmetic and copies ran while one was open for 1% of the time, Pallas kernels for 0%

commit v1 on v0

v1 whole, which is shorter than its diff:
```python
import functools
import math

import jax
import jax.numpy as jnp
from jax import lax
from jax.experimental import pallas as pl
from jax.experimental.pallas import tpu as pltpu
from jax.sharding import PartitionSpec as P

CLASSES = 128
ITERS = 4
MESH = pl.DeviceIdType.MESH
F32 = jnp.float32
BF16 = jnp.bfloat16
NT = (((1,), (1,)), ((), ()))


class Plan:
    def __init__(self, grid, narrow, local_members, local_states, obs_local):
        self.nx, self.nz = grid
        self.narrow = narrow
        self.ny = narrow // 2
        self.ml = local_members
        self.m = local_members * narrow
        self.states = local_states
        self.share = local_states // narrow
        self.obs = obs_local
        self.oshare = obs_local // narrow
        self.nb = self.m // 128
        self.blocks = [(i, j) for i in range(self.nb) for j in range(i, self.nb)]
        self.half = len(self.blocks) // 2
        self.peers = self.nx * self.ny
        self.rows = self.half * 128 // self.peers
        self.tall = self.rows + 16
        self.strip = min(256, self.m)
        assert self.half * 2 == len(self.blocks) and self.rows % 16 == 0
        assert local_members == 128 and self.rows * self.peers == self.half * 128


def segments(plan, pos):
    out, row = [], pos * 128
    while row < (pos + 1) * 128:
        piece, inside = divmod(row, plan.rows)
        count = min(plan.rows - inside, (pos + 1) * 128 - row)
        out.append((piece, inside, row - pos * 128, count))
        row += count
    return out


def resplit(tail, nb):
    total = tail[:nb] + tail[nb : 2 * nb]
    high = total.astype(BF16).astype(F32)
    rest = [high, total - high]
    if 2 * nb < 16:
        rest.append(jnp.zeros((16 - 2 * nb, 128), F32))
    return jnp.concatenate(rest, axis=0)


def kernel(plan, owner, infl, oblk, ens, value, std, out, ens_v, gat, robs, scaled, part, corebuf, chipsum, xybuf,
           zbuf, tailbuf, prow, agbuf, gram, prod, mix, est, estb, raw, anom, tmat, stage, load_sem, obs_s, obs_r,
           core_s, core_r, xy_s, xy_r, z_s, z_r, ag_s, ag_r, fw_s, fw_r, raw_s, raw_r, own_sem, out_s, out_r):
    p = plan
    n = lax.axis_index("narrow")
    w = lax.axis_index("wide")
    x, z = lax.div(w, p.nz), lax.rem(w, p.nz)
    y, c = lax.div(n, 2), lax.rem(n, 2)
    q0 = x * p.ny + y
    root_scale = math.sqrt(p.m - 1)

    def copy_to(src, dst, send, recv, device):
        return pltpu.make_async_remote_copy(
            src_ref=src, dst_ref=dst, send_sem=send, recv_sem=recv, device_id=device, device_id_type=MESH
        )

    def near(t):
        return lax.rem(n + t, p.narrow)

    def along(t):
        return lax.rem(z + t, p.nz)

    def plane(t):
        return lax.rem(q0 + t, p.peers)

    def plane_id(q):
        return (lax.div(q, p.ny) * p.nz + z, lax.rem(q, p.ny) * 2 + c)

    sibling = (w, n + 1 - 2 * c)

    def load_block(b):
        cols = pl.ds(pl.multiple_of(b * 128, 128), 128)
        return pltpu.make_async_copy(ens.at[:, cols], ens_v.at[b], load_sem)

    count = p.states // 128
    lax.fori_loop(0, count, lambda b, carry: (load_block(b).start(), carry)[1], 0)

    barrier = pltpu.get_barrier_semaphore()
    greeted = 0
    for t in range(1, p.narrow):
        pl.semaphore_signal(barrier, inc=1, device_id=(w, near(t)), device_id_type=MESH)
        greeted += 1
    for t in range(1, p.nz):
        pl.semaphore_signal(barrier, inc=1, device_id=(x * p.nz + along(t), n), device_id_type=MESH)
        greeted += 1
    for dx in range(1, p.nx):
        for dy in range(p.ny):
            there = (lax.rem(x + dx, p.nx) * p.nz + z, lax.rem(y + dy, p.ny) * 2 + c)
            pl.semaphore_signal(barrier, inc=1, device_id=there, device_id_type=MESH)
            greeted += 1

    pltpu.make_async_copy(ens_v, ens_v, load_sem).wait()
    per = p.oshare // 128
    for b in range(p.obs // 128):
        gat[b // per, :, (b % per) * 128 : (b % per) * 128 + 128] = ens_v[oblk[b]]
    pl.semaphore_wait(barrier, greeted)

    def obs_copy(t):
        there = near(t)
        return copy_to(gat.at[there], robs.at[n], obs_s.at[t], obs_r.at[n], (w, there))

    def obs_arrival(t):
        frm = near(t)
        return copy_to(gat.at[frm], robs.at[frm], obs_s.at[t], obs_r.at[frm], (w, frm))

    for t in range(1, p.narrow):
        obs_copy(t).start()
    robs[pl.ds(n, 1)] = gat[pl.ds(n, 1)]
    for t in range(1, p.narrow):
        obs_arrival(t).wait_recv()

    innov = []
    for k in range(per):
        cols = slice(k * 128, k * 128 + 128)
        member = robs[:, :, cols].reshape(p.m, 128).astype(F32)
        mean = jnp.sum(member, axis=0, keepdims=True) / p.m
        ob = n * per + k
        factor = infl[owner[oblk[ob]]]
        sigma = std[pl.ds(ob, 1), :]
        shifted = (factor * (member - mean)).astype(BF16)
        scaled[:, cols] = (shifted.astype(F32) / (sigma * root_scale)).astype(BF16)
        innov.append((value[pl.ds(ob, 1), :] - mean) / sigma)
    innov = jnp.concatenate(innov, axis=1)
    high = innov.astype(BF16).astype(F32)
    middle = (innov - high).astype(BF16).astype(F32)
    low = innov - high - middle
    row_ids = lax.broadcasted_iota(jnp.int32, (16, p.oshare), 0)
    lhs = jnp.where(row_ids == 0, high, jnp.where(row_ids == 1, middle, jnp.where(row_ids == 2, low, 0.0)))
    projected = lax.dot_general(lhs.astype(BF16), scaled[...], NT, preferred_element_type=F32)
    projected = jnp.sum(projected, axis=0, keepdims=True)
    tailbuf[...] = jnp.zeros_like(tailbuf)
    for i in range(p.nb):
        tailbuf[i : i + 1, :] = projected[:, i * 128 : i * 128 + 128]
    tail = resplit(tailbuf[...], p.nb).astype(BF16)
    for h in range(2):
        for piece in range(p.peers):
            part[h, piece, p.rows : p.tall, :] = tail
    index = 0
    for i in range(p.nb):
        rows = lax.dot_general(
            scaled[i * 128 : i * 128 + 128, :], scaled[i * 128 :, :], NT, preferred_element_type=F32
        ).astype(BF16)
        for j in range(i, p.nb):
            h, pos = divmod(index, p.half)
            for piece, inside, start, count in segments(p, pos):
                part[h, piece, inside : inside + count, :] = rows[start : start + count, (j - i) * 128 : (j - i) * 128 + 128]
            index += 1

    core_copy = copy_to(part.at[1 - c], corebuf, core_s, core_r, sibling)
    core_copy.start()
    core_copy.wait_recv()
    tail = part[c, 0, p.rows : p.tall, :].astype(F32) + corebuf[0, p.rows : p.tall, :].astype(F32)
    tail = resplit(tail, p.nb).astype(BF16)

    def chip_add(piece, carry):
        total = part[c, piece, : p.rows, :].astype(F32) + corebuf[piece, : p.rows, :].astype(F32)
        chipsum[piece, : p.rows, :] = total.astype(BF16)
        chipsum[piece, p.rows : p.tall, :] = tail
        return carry

    lax.fori_loop(0, p.peers, chip_add, 0)

    def xy_copy(t):
        there = plane(t)
        return copy_to(chipsum.at[there], xybuf.at[q0], xy_s.at[t], xy_r.at[q0], plane_id(there))

    def xy_arrival(t):
        frm = plane(t)
        return copy_to(chipsum.at[frm], xybuf.at[frm], xy_s.at[t], xy_r.at[frm], plane_id(frm))

    lax.fori_loop(1, p.peers, lambda t, carry: (xy_copy(t).start(), carry)[1], 0)

    def xy_add(t, total):
        xy_arrival(t).wait_recv()
        return total + xybuf[plane(t)].astype(F32)

    total = lax.fori_loop(1, p.peers, xy_add, chipsum[q0].astype(F32))
    zbuf[z, : p.rows, :] = total[: p.rows].astype(BF16)
    zbuf[z, p.rows : p.tall, :] = resplit(total[p.rows :], p.nb).astype(BF16)

    def z_copy(t):
        there = along(t)
        return copy_to(zbuf.at[z], zbuf.at[z], z_s.at[t], z_r.at[z], (x * p.nz + there, n))

    def z_arrival(t):
        frm = along(t)
        return copy_to(zbuf.at[frm], zbuf.at[frm], z_s.at[t], z_r.at[frm], (x * p.nz + frm, n))

    for t in range(1, p.nz):
        z_copy(t).start()
    for t in range(1, p.nz):
        z_arrival(t).wait_recv()
    total = zbuf[0].astype(F32)
    for k in range(1, p.nz):
        total = total + zbuf[k].astype(F32)

    def piece_rows(q):
        return pl.ds(pl.multiple_of(q * p.rows, 16), p.rows)

    agbuf[c, piece_rows(q0), :] = total[: p.rows].astype(BF16)
    for i in range(p.nb):
        prow[:, i * 128 : i * 128 + 128] = total[p.rows + i : p.rows + i + 1] + total[p.rows + p.nb + i : p.rows + p.nb + i + 1]

    def ag_copy(t):
        mine = agbuf.at[c, piece_rows(q0), :]
        return copy_to(mine, mine, ag_s.at[t], ag_r.at[q0], plane_id(plane(t)))

    def ag_arrival(t):
        frm = plane(t)
        slot = agbuf.at[c, piece_rows(frm), :]
        return copy_to(slot, slot, ag_s.at[t], ag_r.at[frm], plane_id(frm))

    def forward(q):
        slot = agbuf.at[c, piece_rows(q), :]
        return copy_to(slot, slot, fw_s.at[q], fw_r.at[q], sibling)

    def forward_arrival(q):
        slot = agbuf.at[1 - c, piece_rows(q), :]
        return copy_to(slot, slot, fw_s.at[q], fw_r.at[q], sibling)

    lax.fori_loop(1, p.peers, lambda t, carry: (ag_copy(t).start(), carry)[1], 0)
    forward(q0).start()

    def pass_on(t, carry):
        ag_arrival(t).wait_recv()
        forward(plane(t)).start()
        return carry

    lax.fori_loop(1, p.peers, pass_on, 0)

    def share_cols(k):
        return pl.ds(pl.multiple_of(k * p.share, 128), p.share)

    def raw_copy(t):
        there = near(t)
        return copy_to(ens.at[:, share_cols(there)], raw.at[n], raw_s.at[t], raw_r.at[n], (w, there))

    def raw_arrival(t):
        frm = near(t)
        return copy_to(ens.at[:, share_cols(frm)], raw.at[frm], raw_s.at[t], raw_r.at[frm], (w, frm))

    for t in range(1, p.narrow):
        raw_copy(t).start()
    own = pltpu.make_async_copy(ens.at[:, share_cols(n)], raw.at[n], own_sem)
    own.start()
    lax.fori_loop(0, p.peers, lambda q, carry: (forward_arrival(q).wait_recv(), carry)[1], 0)

    diag = lax.broadcasted_iota(jnp.int32, (128, 128), 0) == lax.broadcasted_iota(jnp.int32, (128, 128), 1)
    eye = diag.astype(F32)
    square = jnp.zeros((128, 128), F32)
    index = 0
    for i in range(p.nb):
        for j in range(i, p.nb):
            h, pos = divmod(index, p.half)
            block = agbuf[h, pos * 128 : pos * 128 + 128, :]
            wide = block.astype(F32)
            if i == j:
                wide = wide + eye
                block = wide.astype(BF16)
                square = square + wide * wide
            else:
                square = square + 2.0 * (wide * wide)
                gram[j * 128 : j * 128 + 128, i * 128 : i * 128 + 128] = wide.T.astype(BF16)
            gram[i * 128 : i * 128 + 128, j * 128 : j * 128 + 128] = block
            index += 1
    square = jnp.sum(jnp.sum(square, axis=0, keepdims=True), axis=1, keepdims=True)
    frob = jnp.sqrt(square)
    inv = 1.0 / frob

    strips = p.m // p.strip

    def cols_of(s):
        return pl.ds(pl.multiple_of(s * p.strip, 128), p.strip)

    def mm(a, b):
        return jnp.dot(a, b, preferred_element_type=F32)

    def first(s, carry):
        cols = cols_of(s)
        unit = gram[:, cols].astype(F32) * inv
        unit2 = mm(gram[...], gram[:, cols]) * (inv * inv)
        prod[:, cols] = unit2.astype(BF16)
        mix[:, cols] = (0.0625 * unit2 - 0.5625 * unit).astype(BF16)
        est[:, cols] = 1.6875 * unit2 - 2.4375 * unit
        return carry

    def second(s, carry):
        cols = cols_of(s)
        new = est[:, cols] + mm(prod[...], mix[:, cols])
        est[:, cols] = new
        estb[:, cols] = new.astype(BF16)
        return carry

    lax.fori_loop(0, strips, first, 0)
    lax.fori_loop(0, strips, second, 0)
    level = 2.25
    for turn in range(2, ITERS):
        last = turn == ITERS - 1

        def left(s, carry, level=level):
            cols = cols_of(s)
            old = est[:, cols]
            unit_it = gram[:, cols].astype(F32) * (level * inv) + mm(gram[...], estb[:, cols]) * inv
            prod[:, cols] = unit_it.astype(BF16)
            mix[:, cols] = (2.0 * level * old + mm(estb[...], estb[:, cols])).astype(BF16)
            est[:, cols] = 1.5 * old - (0.5 * level * level) * unit_it
            return carry

        def right(s, carry, level=level, last=last):
            cols = cols_of(s)
            new = est[:, cols] - 0.5 * mm(prod[...], mix[:, cols])
            if last:
                row_ids = lax.broadcasted_iota(jnp.int32, (p.m, p.strip), 0)
                col_ids = lax.broadcasted_iota(jnp.int32, (p.m, p.strip), 1) + s * p.strip
                est[:, cols] = new + jnp.where(row_ids == col_ids, 1.5 * level, 0.0)
            else:
                est[:, cols] = new
                estb[:, cols] = new.astype(BF16)
            return carry

        lax.fori_loop(0, strips, left, 0)
        lax.fori_loop(0, strips, right, 0)
        level = 1.5 * level

    inv_root = lax.rsqrt(frob)

    def shift_rows(s, total):
        rows = pl.ds(pl.multiple_of(s * 128, 128), 128)
        block = est[rows, :]
        midway = jnp.sum(block * prow[...], axis=1, keepdims=True)
        return total + jnp.sum(block * midway, axis=0, keepdims=True)

    shift = lax.fori_loop(0, p.m // 128, shift_rows, jnp.zeros((1, p.m), F32))
    shift = shift * (inv / root_scale)

    def transform_rows(s, carry):
        rows = pl.ds(pl.multiple_of(s * 128, 128), 128)
        tmat[rows, :] = (est[rows, :] * inv_root + shift).astype(BF16)
        return carry

    lax.fori_loop(0, p.m // 128, transform_rows, 0)

    for t in range(1, p.narrow):
        raw_arrival(t).wait_recv()
    own.wait()
    state_mean = jnp.zeros((1, p.share), F32)
    for k in range(p.narrow):
        state_mean = state_mean + jnp.sum(raw[k].astype(F32), axis=0, keepdims=True)
    state_mean = state_mean / p.m
    factors = [
        jnp.full((1, 128), infl[owner[n * (p.share // 128) + b]], F32) for b in range(p.share // 128)
    ]
    factors = jnp.concatenate(factors, axis=1)
    for k in range(p.narrow):
        anom[k * 128 : k * 128 + 128, :] = (factors * (raw[k].astype(F32) - state_mean)).astype(BF16)

    def out_copy(dy, core):
        there = lax.rem(y + dy, p.ny) * 2 + core
        return copy_to(
            stage.at[dy, pl.ds(core * 128, 128), :], out.at[:, share_cols(n)], out_s.at[dy, core],
            out_r.at[n], (w, there)
        )

    def out_arrival(frm):
        return copy_to(
            stage.at[0, pl.ds(0, 128), :], out.at[:, share_cols(frm)], out_s.at[0, 0], out_r.at[frm], (w, frm)
        )

    def analyse(dy):
        rows = pl.ds(pl.multiple_of(lax.rem(y + dy, p.ny) * 256, 256), 256)
        stage[dy] = (state_mean + mm(tmat[rows, :], anom[...])).astype(BF16)

    order = sorted(range(1, p.ny), key=lambda d: -min(d, p.ny - d))
    for dy in order:
        analyse(dy)
        for core in range(2):
            out_copy(dy, core).start()
    analyse(0)
    to_sibling = copy_to(
        stage.at[0, pl.ds(pl.multiple_of((1 - c) * 128, 128), 128), :], out.at[:, share_cols(n)], out_s.at[0, 0], out_r.at[n], sibling
    )
    to_sibling.start()
    keep = pltpu.make_async_copy(
        stage.at[0, pl.ds(pl.multiple_of(c * 128, 128), 128), :], out.at[:, share_cols(n)], own_sem
    )
    keep.start()

    for t in range(1, p.narrow):
        out_arrival(near(t)).wait_recv()
    keep.wait()
    to_sibling.wait_send()
    for dy in order:
        for core in range(2):
            out_copy(dy, core).wait_send()
    for t in range(1, p.narrow):
        obs_copy(t).wait_send()
        raw_copy(t).wait_send()
    core_copy.wait_send()
    for t in range(1, p.nz):
        z_copy(t).wait_send()

    def drain(t, carry):
        xy_copy(t).wait_send()
        ag_copy(t).wait_send()
        return carry

    lax.fori_loop(1, p.peers, drain, 0)
    lax.fori_loop(0, p.peers, lambda q, carry: (forward(q).wait_send(), carry)[1], 0)


def on_device(grid, narrow, ensemble, owner, inflation, obs_block, obs_value, obs_std):
    p = Plan(grid, narrow, *ensemble.shape, obs_value.shape[0])
    dma = pltpu.SemaphoreType.DMA
    vmem, smem = pl.BlockSpec(memory_space=pltpu.VMEM), pl.BlockSpec(memory_space=pltpu.SMEM)
    anywhere = pl.BlockSpec(memory_space=pl.ANY)
    square = (p.m, p.m)
    scratch = [
        pltpu.VMEM((p.states // 128, p.ml, 128), BF16),
        pltpu.VMEM((p.narrow, p.ml, p.oshare), BF16),
        pltpu.VMEM((p.narrow, p.ml, p.oshare), BF16),
        pltpu.VMEM((p.m, p.oshare), BF16),
        pltpu.VMEM((2, p.peers, p.tall, 128), BF16),
        pltpu.VMEM((p.peers, p.tall, 128), BF16),
        pltpu.VMEM((p.peers, p.tall, 128), BF16),
        pltpu.VMEM((p.peers, p.tall, 128), BF16),
        pltpu.VMEM((p.nz, p.tall, 128), BF16),
        pltpu.VMEM((16, 128), F32),
        pltpu.VMEM((1, p.m), F32),
        pltpu.VMEM((2, p.peers * p.rows, 128), BF16),
        pltpu.VMEM(square, BF16),
        pltpu.VMEM(square, BF16),
        pltpu.VMEM(square, BF16),
        pltpu.VMEM(square, F32),
        pltpu.VMEM(square, BF16),
        pltpu.VMEM((p.narrow, p.ml, p.share), BF16),
        pltpu.VMEM((p.m, p.share), BF16),
        pltpu.VMEM(square, BF16),
        pltpu.VMEM((p.ny, 256, p.share), BF16),
        dma, dma((p.narrow,)), dma((p.narrow,)),
        dma, dma,
        dma((p.peers,)), dma((p.peers,)),
        dma((p.nz,)), dma((p.nz,)),
        dma((p.peers,)), dma((p.peers,)),
        dma((p.peers,)), dma((p.peers,)),
        dma((p.narrow,)), dma((p.narrow,)),
        dma, dma((p.ny, 2)), dma((p.narrow,)),
    ]
    return pl.pallas_call(
        functools.partial(kernel, p),
        out_shape=jax.ShapeDtypeStruct(ensemble.shape, BF16),
        in_specs=[smem, smem, smem, anywhere, vmem, vmem],
        out_specs=anywhere,
        scratch_shapes=scratch,
        compiler_params=pltpu.CompilerParams(
            collective_id=0, has_side_effects=True, vmem_limit_bytes=56 * 1024 * 1024
        ),
        name="etkf",
    )(owner, inflation, obs_block, ensemble, obs_value.reshape(-1, 128), obs_std.reshape(-1, 128))


def solution(mesh):
    wide, narrow = mesh.shape["wide"], mesh.shape["narrow"]
    grid = (4, wide // 4) if wide >= 16 else (2, wide // 2)
    return jax.shard_map(
        functools.partial(on_device, grid, narrow),
        mesh=mesh,
        in_specs=(P("narrow", "wide"), P("wide"), P(), P("wide"), P("wide"), P("wide")),
        out_specs=P("narrow", "wide"),
        check_vma=False,
    )
```

time: 805 us -> 109 us (0.14)
  waiting for transfers between devices: 487 us -> 0 us
  blocking collectives: 209 us -> 0 us
  Pallas kernels: 0 us -> 106 us
  matrix products: 39 us -> 0 us
  starting transfers between devices: 21.9 us -> 0 us
  other arithmetic: 18.9 us -> 0 us
  between operations: 14.7 us -> 0.01 us
  local copies, waits for them, and re-layouts: 13.5 us -> 3.1 us
    psum x1 -> x0, waiting for transfers between devices: 268 us -> none  [on_device(): lax.psum((gram_part, projected_part), ('wide', 'narrow'))]
    all_gather x4 -> x0, waiting for transfers between devices: 192 us -> none  [the longest x3 158 us: on_device(): iterate_all = lax.all_gather(iterate, 'wide', axis=0, tiled=True)]
    pallas_call x0 -> x1, Pallas kernels: none -> 106 us  [on_device(): pl.pallas_call(functools.partial(kernel, p), out_shape=jax.ShapeDtypeStru...]
    psum x2 -> x0, blocking collectives: 102 us -> none  [the longest x1 78.5 us: on_device(): lax.psum((gram_part, projected_part), ('wide', 'narrow'))]
    unnamed x1 -> x0, blocking collectives: 56 us -> none
    all_to_all x2 -> x0, blocking collectives: 50.4 us -> none  [the longest x1 35.1 us: on_device(): lax.all_to_all(analysis_share, 'narrow', split_axis=0, concat_axis=1, til...]
    dot_general x14 -> x0, matrix products: 39 us -> none  [the longest x3 14.7 us: on_device(): product_one = jnp.dot(unit_rows, iterate_all, precision=HIGH)]
    all_to_all x1 -> x0, waiting for transfers between devices: 26.3 us -> none  [on_device(): lax.all_to_all(anomaly, 'narrow', split_axis=1, concat_axis=0, tiled=True)]
  transfers between devices with their start and end apart: 6 -> 0, of which waited for: 5 -> 0; matrix products, arithmetic and copies ran while one was open for 1% -> 0% of each run, Pallas kernels for 0% -> 0%
where the time goes in v1:
time: 109 us
  Pallas kernels  106 us (97%)
  local copies, waits for them, and re-layouts  3.1 us (3%)
    pallas_call x1, Pallas kernels, on_device(): pl.pallas_call(functools.partial(kernel, p), out_shape=jax.ShapeDtypeStru...  106 us
    unnamed x1, local copies, waits for them, and re-layouts  3.1 us

profile of v1, /device:TPU:1, one launch (start us, length us, event | category | flops | bytes accessed | tf_op | source)
XLA Modules:
  0.0 108.9 jit_solution(14486011678056304262)
XLA Ops:
  0.0 105.8 %etkf.1 = bf16[128,8192]{1,0:T(8,128)(2,1)} custom-call(s32[64]{0:T(128)} %owner.1, f32[256]{0:T(256)} %infl.1, s32[16]{0:T(128)} %oblk.1, bf16[128,8192]{1,0:T(8,128)(2,1)} %ens.1, f32[16,128]{1,0:T(8,128)} %bitcast.2, f32[16,128]{1,0:T(8,128)} %bitcast.3), custom_call_target="tpu_custom_call" | custom-call | tf_op jit(solution)/shard_map/etkf/pallas_call | solution.py:467
  105.8 3.1 %copy.8 = bf16[128,8192]{1,0:T(8,128)(2,1)} copy(bf16[128,8192]{1,0:T(8,128)(2,1)} %etkf.1) | data formatting | bytes 4194304

commit v2 on v1

v2 whole, which is shorter than its diff:
```python
import functools
import math

import jax
import jax.numpy as jnp
from jax import lax
from jax.experimental import pallas as pl
from jax.experimental.pallas import tpu as pltpu
from jax.sharding import PartitionSpec as P

CLASSES = 128
MESH = pl.DeviceIdType.MESH
F32 = jnp.float32
BF16 = jnp.bfloat16
NT = (((1,), (1,)), ((), ()))
RAW_AT = ((None, None, 0, 0), (4, 4, 4, 4), (0, 1, 2, 4))


class Plan:
    def __init__(self, grid, narrow, local_members, local_states, obs_local):
        self.nx, self.nz = grid
        self.narrow = narrow
        self.ny = narrow // 2
        self.ml = local_members
        self.m = local_members * narrow
        self.states = local_states
        self.share = local_states // narrow
        self.obs = obs_local
        self.oshare = obs_local // narrow
        self.nb = self.m // 128
        self.blocks = [(i, j) for i in range(self.nb) for j in range(i, self.nb)]
        self.half = len(self.blocks) // 2
        self.peers = self.nx * self.ny
        tiles = self.half * 8
        self.ra = tiles * 2 // 3 // self.peers * 16
        self.rb = (tiles * 16 - self.ra * self.peers) // self.nz
        self.tb = self.rb + 16
        self.base = self.ra * self.peers
        self.strip = min(256, self.m)
        assert self.half * 2 == len(self.blocks) and self.rb % 16 == 0
        assert local_members == 128 and self.base + self.rb * self.nz == self.half * 128
        self.near = sorted(((d, f) for d in range(self.ny) for f in range(2) if d + f), key=lambda k: -min(k[0], self.ny - k[0]))


def segments(plan, pos):
    out, row = [], pos * 128
    while row < (pos + 1) * 128:
        first = row < plan.base
        size = plan.ra if first else plan.rb
        piece, inside = divmod(row if first else row - plan.base, size)
        count = min(size - inside, (pos + 1) * 128 - row)
        out.append((first, piece, inside, row - pos * 128, count))
        row += count
    return out


def resplit(tail, nb):
    total = tail[:nb] + tail[nb : 2 * nb]
    high = total.astype(BF16).astype(F32)
    rest = [high, total - high]
    if 2 * nb < 16:
        rest.append(jnp.zeros((16 - 2 * nb, 128), F32))
    return jnp.concatenate(rest, axis=0)


def kernel(plan, owner, infl, oblk, ens, value, std, out, ens_v, gat, robs, scaled, part_a, part_b, core_a, core_b, chip_a,
           chip_b, xy_a, z_b, z_a, x_b, y_b, tailbuf, prow, agbuf, gram, prod, mix, est, estb, more, moreb, raw, anom, tmat, stage,
           load_sem, obs_s, obs_r, core_s, core_r, xa_s, xa_r, zb_s, zb_r, za_s, za_r, xb_s, xb_r, yb_s, yb_r, ga_s, ga_r, gb_s, gb_r,
           fa_s, fa_r, fb_s, fb_r, raw_s, raw_r, own_sem, out_s, out_r):
    p = plan
    n = lax.axis_index("narrow")
    w = lax.axis_index("wide")
    x, z = lax.div(w, p.nz), lax.rem(w, p.nz)
    y, c = lax.div(n, 2), lax.rem(n, 2)
    q0 = x * p.ny + y
    root_scale = math.sqrt(p.m - 1)
    pending = []

    def copy_to(src, dst, send, recv, device):
        return pltpu.make_async_remote_copy(
            src_ref=src, dst_ref=dst, send_sem=send, recv_sem=recv, device_id=device, device_id_type=MESH
        )

    def near(k):
        return lax.rem(y + k[0], p.ny) * 2 + (1 - c if k[1] else c)

    def along(t):
        return lax.rem(z + t, p.nz)

    def along_id(k):
        return (x * p.nz + k, n)

    def plane(t):
        return lax.rem(q0 + t, p.peers)

    def plane_id(q):
        return (lax.div(q, p.ny) * p.nz + z, lax.rem(q, p.ny) * 2 + c)

    sibling = (w, n + 1 - 2 * c)

    def each(count, step):
        def body(t, carry):
            step(t)
            return carry

        lax.fori_loop(1, count, body, 0)

    def finish(items):
        for item in items:
            if isinstance(item, tuple):
                each(item[0], lambda t: item[1](t).wait_send())
            else:
                item.wait_send()

    def load_block(b):
        cols = pl.ds(pl.multiple_of(b * 128, 128), 128)
        return pltpu.make_async_copy(ens.at[:, cols], ens_v.at[b], load_sem)

    count = p.states // 128
    lax.fori_loop(0, count, lambda b, carry: (load_block(b).start(), carry)[1], 0)

    barrier = pltpu.get_barrier_semaphore()
    greeted = 0
    for k in p.near:
        pl.semaphore_signal(barrier, inc=1, device_id=(w, near(k)), device_id_type=MESH)
        greeted += 1
    for t in range(1, p.nz):
        pl.semaphore_signal(barrier, inc=1, device_id=along_id(along(t)), device_id_type=MESH)
        greeted += 1
    for dx in range(1, p.nx):
        for dy in range(p.ny):
            there = (lax.rem(x + dx, p.nx) * p.nz + z, lax.rem(y + dy, p.ny) * 2 + c)
            pl.semaphore_signal(barrier, inc=1, device_id=there, device_id_type=MESH)
            greeted += 1

    pltpu.make_async_copy(ens_v, ens_v, load_sem).wait()
    per = p.oshare // 128
    for b in range(p.obs // 128):
        gat[b // per, :, (b % per) * 128 : (b % per) * 128 + 128] = ens_v[oblk[b]]
    pl.semaphore_wait(barrier, greeted)

    def obs_copy(k):
        there = near(k)
        return copy_to(gat.at[there], robs.at[n], obs_s.at[2 * k[0] + k[1]], obs_r.at[n], (w, there))

    def obs_arrival(k):
        frm = near(k)
        return copy_to(gat.at[frm], robs.at[frm], obs_s.at[0], obs_r.at[frm], (w, frm))

    for k in p.near:
        obs_copy(k).start()
        pending.append(obs_copy(k))
    robs[pl.ds(n, 1)] = gat[pl.ds(n, 1)]
    for k in p.near:
        obs_arrival(k).wait_recv()

    def share_cols(k):
        return pl.ds(pl.multiple_of(k * p.share, 128), p.share)

    def half_cols(k, h):
        return pl.ds(pl.multiple_of(k * p.share + h * (p.share // 2), 128), p.share // 2)

    def half_slot(k, h):
        return raw.at[k, :, pl.ds(h * (p.share // 2), p.share // 2)]

    def raw_copy(k, h):
        there = near(k)
        src = ens.at[:, half_cols(there, h)]
        return copy_to(src, half_slot(n, h), raw_s.at[2 * k[0] + k[1], h], raw_r.at[n, h], (w, there))

    def raw_arrival(k, h):
        frm = near(k)
        return copy_to(ens.at[:, half_cols(frm, h)], half_slot(frm, h), raw_s.at[0, 0], raw_r.at[frm, h], (w, frm))

    def raw_start(when):
        for k in p.near:
            for h in range(2):
                if RAW_AT[min(k[0], p.ny - k[0])][2 * k[1] + h] == when:
                    raw_copy(k, h).start()
                    pending.append(raw_copy(k, h))

    own = pltpu.make_async_copy(ens.at[:, share_cols(n)], raw.at[n], own_sem)
    own.start()
    raw_start(0)

    innov = []
    for k in range(per):
        cols = slice(k * 128, k * 128 + 128)
        member = robs[:, :, cols].reshape(p.m, 128).astype(F32)
        mean = jnp.sum(member, axis=0, keepdims=True) / p.m
        ob = n * per + k
        factor = infl[owner[oblk[ob]]]
        sigma = std[pl.ds(ob, 1), :]
        shifted = (factor * (member - mean)).astype(BF16)
        scaled[:, cols] = (shifted.astype(F32) / (sigma * root_scale)).astype(BF16)
        innov.append((value[pl.ds(ob, 1), :] - mean) / sigma)
    innov = jnp.concatenate(innov, axis=1)
    high = innov.astype(BF16).astype(F32)
    middle = (innov - high).astype(BF16).astype(F32)
    low = innov - high - middle
    row_ids = lax.broadcasted_iota(jnp.int32, (16, p.oshare), 0)
    lhs = jnp.where(row_ids == 0, high, jnp.where(row_ids == 1, middle, jnp.where(row_ids == 2, low, 0.0)))
    projected = lax.dot_general(lhs.astype(BF16), scaled[...], NT, preferred_element_type=F32)
    projected = jnp.sum(projected, axis=0, keepdims=True)
    tailbuf[...] = jnp.zeros_like(tailbuf)
    for i in range(p.nb):
        tailbuf[i : i + 1, :] = projected[:, i * 128 : i * 128 + 128]
    tail = resplit(tailbuf[...], p.nb).astype(BF16)
    for h in range(2):
        part_b[h, 0, p.rb :, :] = tail
        for k in range(1, p.nz):
            part_b[h, k, p.rb :, :] = jnp.zeros_like(tail)
    index = 0
    for i in range(p.nb):
        rows = lax.dot_general(
            scaled[i * 128 : i * 128 + 128, :], scaled[i * 128 :, :], NT, preferred_element_type=F32
        ).astype(BF16)
        for j in range(i, p.nb):
            h, pos = divmod(index, p.half)
            for first, piece, inside, start, count in segments(p, pos):
                ref = part_a if first else part_b
                ref[h, piece, inside : inside + count, :] = rows[start : start + count, (j - i) * 128 : (j - i) * 128 + 128]
            index += 1

    core_copy_b = copy_to(part_b.at[1 - c], core_b, core_s.at[0], core_r.at[0], sibling)
    core_copy_a = copy_to(part_a.at[1 - c], core_a, core_s.at[1], core_r.at[1], sibling)
    core_copy_b.start()
    core_copy_a.start()
    pending += [core_copy_a, core_copy_b]

    def zb_copy(t):
        there = along(t)
        return copy_to(chip_b.at[there], z_b.at[z], zb_s.at[t], zb_r.at[z], along_id(there))

    def zb_arrival(t):
        frm = along(t)
        return copy_to(chip_b.at[frm], z_b.at[frm], zb_s.at[0], zb_r.at[frm], along_id(frm))

    def xa_copy(t):
        there = plane(t)
        return copy_to(chip_a.at[there], xy_a.at[q0], xa_s.at[t], xa_r.at[q0], plane_id(there))

    def xa_arrival(t):
        frm = plane(t)
        return copy_to(chip_a.at[frm], xy_a.at[frm], xa_s.at[0], xa_r.at[frm], plane_id(frm))

    def add_b(k, carry):
        total = part_b[c, k, : p.rb, :].astype(F32) + core_b[k, : p.rb, :].astype(F32)
        chip_b[k, : p.rb, :] = total.astype(BF16)
        chip_b[k, p.rb :, :] = tail
        return carry

    def add_a(k, carry):
        chip_a[k] = (part_a[c, k].astype(F32) + core_a[k].astype(F32)).astype(BF16)
        return carry

    core_copy_b.wait_recv()
    tail = resplit(part_b[c, 0, p.rb :, :].astype(F32) + core_b[0, p.rb :, :].astype(F32), p.nb).astype(BF16)
    lax.fori_loop(0, p.nz, add_b, 0)
    each(p.nz, lambda t: zb_copy(t).start())
    core_copy_a.wait_recv()
    lax.fori_loop(0, p.peers, add_a, 0)
    each(p.peers, lambda t: xa_copy(t).start())
    pending += [(p.nz, zb_copy), (p.peers, xa_copy)]
    raw_start(1)

    def za_copy(t):
        return copy_to(z_a.at[z], z_a.at[z], za_s.at[t], za_r.at[z], along_id(along(t)))

    def za_arrival(t):
        frm = along(t)
        return copy_to(z_a.at[frm], z_a.at[frm], za_s.at[0], za_r.at[frm], along_id(frm))

    def x_id(t):
        return (lax.rem(x + t, p.nx) * p.nz + z, n)

    def y_id(t):
        return (w, lax.rem(y + t, p.ny) * 2 + c)

    def xb_copy(t):
        return copy_to(x_b.at[x], x_b.at[x], xb_s.at[t], xb_r.at[x], x_id(t))

    def xb_arrival(t):
        frm = lax.rem(x + t, p.nx)
        return copy_to(x_b.at[frm], x_b.at[frm], xb_s.at[0], xb_r.at[frm], x_id(t))

    def yb_copy(t):
        return copy_to(y_b.at[y], y_b.at[y], yb_s.at[t], yb_r.at[y], y_id(t))

    def yb_arrival(t):
        frm = lax.rem(y + t, p.ny)
        return copy_to(y_b.at[frm], y_b.at[frm], yb_s.at[0], yb_r.at[frm], y_id(t))

    def take(arrival, ref, turn):
        def body(t, total):
            arrival(t).wait_recv()
            return total + ref[turn(t)].astype(F32)

        return body

    def put_b(ref, at, total):
        ref[at, : p.rb, :] = total[: p.rb].astype(BF16)
        ref[at, p.rb :, :] = resplit(total[p.rb :], p.nb).astype(BF16)

    put_b(x_b, x, lax.fori_loop(1, p.nz, take(zb_arrival, z_b, along), chip_b[z].astype(F32)))
    each(p.nx, lambda t: xb_copy(t).start())
    total = lax.fori_loop(1, p.peers, take(xa_arrival, xy_a, plane), chip_a[q0].astype(F32))
    z_a[z] = total.astype(BF16)
    each(p.nz, lambda t: za_copy(t).start())
    put_b(y_b, y, lax.fori_loop(1, p.nx, take(xb_arrival, x_b, lambda t: lax.rem(x + t, p.nx)), x_b[x].astype(F32)))
    each(p.ny, lambda t: yb_copy(t).start())
    pending += [(p.nx, xb_copy), (p.nz, za_copy), (p.ny, yb_copy)]
    raw_start(2)

    def rows_a(q):
        return pl.ds(pl.multiple_of(q * p.ra, 16), p.ra)

    def rows_b(k):
        return pl.ds(pl.multiple_of(p.base + k * p.rb, 16), p.rb)

    def ga_copy(t):
        mine = agbuf.at[c, rows_a(q0), :]
        return copy_to(mine, mine, ga_s.at[t], ga_r.at[q0], plane_id(plane(t)))

    def ga_arrival(t):
        slot = agbuf.at[c, rows_a(plane(t)), :]
        return copy_to(slot, slot, ga_s.at[0], ga_r.at[plane(t)], plane_id(plane(t)))

    def gb_copy(t):
        mine = agbuf.at[c, rows_b(z), :]
        return copy_to(mine, mine, gb_s.at[t], gb_r.at[z], along_id(along(t)))

    def gb_arrival(t):
        slot = agbuf.at[c, rows_b(along(t)), :]
        return copy_to(slot, slot, gb_s.at[0], gb_r.at[along(t)], along_id(along(t)))

    def fa_copy(t):
        slot = agbuf.at[c, rows_a(plane(t)), :]
        return copy_to(slot, slot, fa_s.at[t], fa_r.at[plane(t)], sibling)

    def fb_copy(t):
        slot = agbuf.at[c, rows_b(along(t)), :]
        return copy_to(slot, slot, fb_s.at[t], fb_r.at[along(t)], sibling)

    def fa_arrival(q):
        slot = agbuf.at[1 - c, rows_a(q), :]
        return copy_to(slot, slot, fa_s.at[0], fa_r.at[q], sibling)

    def fb_arrival(k):
        slot = agbuf.at[1 - c, rows_b(k), :]
        return copy_to(slot, slot, fb_s.at[0], fb_r.at[k], sibling)

    total = lax.fori_loop(1, p.nz, take(za_arrival, z_a, along), z_a[z].astype(F32))
    agbuf[c, rows_a(q0), :] = total.astype(BF16)
    each(p.peers, lambda t: ga_copy(t).start())
    fa_copy(0).start()
    total = lax.fori_loop(1, p.ny, take(yb_arrival, y_b, lambda t: lax.rem(y + t, p.ny)), y_b[y].astype(F32))
    agbuf[c, rows_b(z), :] = total[: p.rb].astype(BF16)
    each(p.nz, lambda t: gb_copy(t).start())
    fb_copy(0).start()
    pending += [(p.peers, ga_copy), (p.nz, gb_copy), (p.peers, fa_copy), (p.nz, fb_copy), fa_copy(0), fb_copy(0)]
    raw_start(3)
    for i in range(p.nb):
        row = total[p.rb + i : p.rb + i + 1] + total[p.rb + p.nb + i : p.rb + p.nb + i + 1]
        prow[:, i * 128 : i * 128 + 128] = row

    def pass_a(t):
        ga_arrival(t).wait_recv()
        fa_copy(t).start()

    def pass_b(t):
        gb_arrival(t).wait_recv()
        fb_copy(t).start()

    each(p.nz, pass_b)
    each(p.peers, pass_a)
    raw_start(4)
    lax.fori_loop(0, p.nz, lambda k, carry: (fb_arrival(k).wait_recv(), carry)[1], 0)
    lax.fori_loop(0, p.peers, lambda q, carry: (fa_arrival(q).wait_recv(), carry)[1], 0)

    diag = lax.broadcasted_iota(jnp.int32, (128, 128), 0) == lax.broadcasted_iota(jnp.int32, (128, 128), 1)
    eye = diag.astype(F32)
    square = jnp.zeros((128, 128), F32)
    index = 0
    for i in range(p.nb):
        for j in range(i, p.nb):
            h, pos = divmod(index, p.half)
            block = agbuf[h, pos * 128 : pos * 128 + 128, :]
            wide = block.astype(F32)
            if i == j:
                wide = wide + eye
                block = wide.astype(BF16)
                square = square + wide * wide
            else:
                square = square + 2.0 * (wide * wide)
                gram[j * 128 : j * 128 + 128, i * 128 : i * 128 + 128] = wide.T.astype(BF16)
            gram[i * 128 : i * 128 + 128, j * 128 : j * 128 + 128] = block
            index += 1
    square = jnp.sum(jnp.sum(square, axis=0, keepdims=True), axis=1, keepdims=True)
    frob = jnp.sqrt(square)
    inv = 1.0 / frob

    strips = p.m // p.strip

    def mm(a, b):
        return jnp.dot(a, b, preferred_element_type=F32)

    def put(ref, s, value):
        cols = slice(s * p.strip, (s + 1) * p.strip)
        value = value.astype(ref.dtype)
        ref[: (s + 1) * p.strip, cols] = value
        if s > 0:
            ref[cols, : s * p.strip] = value[: s * p.strip].T

    def corner(s):
        return slice(0, (s + 1) * p.strip), slice(s * p.strip, (s + 1) * p.strip)

    for s in range(strips):
        rows, cols = corner(s)
        unit = gram[rows, cols].astype(F32) * inv
        unit2 = mm(gram[rows, :], gram[:, cols]) * (inv * inv)
        put(prod, s, unit2)
        put(mix, s, 0.0625 * unit2 - 0.5625 * unit)
        est[rows, cols] = 1.6875 * unit2 - 2.4375 * unit
    for s in range(strips):
        rows, cols = corner(s)
        new = est[rows, cols] + mm(prod[rows, :], mix[:, cols])
        est[rows, cols] = new
        put(estb, s, new)
    for s in range(strips):
        rows, cols = corner(s)
        half = gram[rows, cols].astype(F32) * (2.25 * inv) + mm(gram[rows, :], estb[:, cols]) * inv
        more[rows, cols] = half
        put(prod, s, half)
    for s in range(strips):
        rows, cols = corner(s)
        unit = 2.25 * more[rows, cols] + mm(prod[rows, :], estb[:, cols])
        more[rows, cols] = unit
        put(mix, s, unit)
    for s in range(strips):
        rows, cols = corner(s)
        unit = more[rows, cols]
        unit2 = mm(mix[rows, :], mix[:, cols])
        put(prod, s, unit2)
        put(moreb, s, 0.0625 * unit2 - 0.5625 * unit)
        more[rows, cols] = 1.6875 * unit2 - 2.4375 * unit
    for s in range(strips):
        rows, cols = corner(s)
        new = more[rows, cols] + mm(prod[rows, :], moreb[:, cols])
        put(mix, s, new)
        est[rows, cols] = 2.25 * (est[rows, cols] + new)
    for s in range(strips):
        rows, cols = corner(s)
        new = est[rows, cols] + mm(estb[rows, :], mix[:, cols])
        row_ids = lax.broadcasted_iota(jnp.int32, new.shape, 0)
        col_ids = lax.broadcasted_iota(jnp.int32, new.shape, 1) + s * p.strip
        put(est, s, new + jnp.where(row_ids == col_ids, 2.25 * 2.25, 0.0))

    inv_root = lax.rsqrt(frob)

    def shift_rows(s, total):
        rows = pl.ds(pl.multiple_of(s * 128, 128), 128)
        block = est[rows, :]
        midway = jnp.sum(block * prow[...], axis=1, keepdims=True)
        return total + jnp.sum(block * midway, axis=0, keepdims=True)

    shift = lax.fori_loop(0, p.m // 128, shift_rows, jnp.zeros((1, p.m), F32))
    shift = shift * (inv / root_scale)

    def transform_rows(s, carry):
        rows = pl.ds(pl.multiple_of(s * 128, 128), 128)
        tmat[rows, :] = (est[rows, :] * inv_root + shift).astype(BF16)
        return carry

    lax.fori_loop(0, p.m // 128, transform_rows, 0)

    for k in p.near:
        raw_arrival(k, 0).wait_recv()
        raw_arrival(k, 1).wait_recv()
    own.wait()
    state_mean = jnp.zeros((1, p.share), F32)
    for k in range(p.narrow):
        state_mean = state_mean + jnp.sum(raw[k].astype(F32), axis=0, keepdims=True)
    state_mean = state_mean / p.m
    factors = [
        jnp.full((1, 128), infl[owner[n * (p.share // 128) + b]], F32) for b in range(p.share // 128)
    ]
    factors = jnp.concatenate(factors, axis=1)
    for k in range(p.narrow):
        anom[k * 128 : k * 128 + 128, :] = (factors * (raw[k].astype(F32) - state_mean)).astype(BF16)

    def out_copy(dy, core):
        there = lax.rem(y + dy, p.ny) * 2 + core
        return copy_to(
            stage.at[dy, pl.ds(core * 128, 128), :], out.at[:, share_cols(n)], out_s.at[dy, core],
            out_r.at[n], (w, there)
        )

    def out_arrival(frm):
        return copy_to(
            stage.at[0, pl.ds(0, 128), :], out.at[:, share_cols(frm)], out_s.at[0, 0], out_r.at[frm], (w, frm)
        )

    def analyse(dy):
        rows = pl.ds(pl.multiple_of(lax.rem(y + dy, p.ny) * 256, 256), 256)
        stage[dy] = (state_mean + mm(tmat[rows, :], anom[...])).astype(BF16)

    order = sorted(range(1, p.ny), key=lambda d: -min(d, p.ny - d))
    for dy in order:
        analyse(dy)
        for core in range(2):
            out_copy(dy, core).start()
    analyse(0)
    to_sibling = copy_to(
        stage.at[0, pl.ds(pl.multiple_of((1 - c) * 128, 128), 128), :], out.at[:, share_cols(n)], out_s.at[0, 0], out_r.at[n], sibling
    )
    to_sibling.start()
    keep = pltpu.make_async_copy(
        stage.at[0, pl.ds(pl.multiple_of(c * 128, 128), 128), :], out.at[:, share_cols(n)], own_sem
    )
    keep.start()

    for k in p.near:
        out_arrival(near(k)).wait_recv()
    keep.wait()
    pending.append(to_sibling)
    pending += [out_copy(dy, core) for dy in order for core in range(2)]
    finish(pending)


def on_device(grid, narrow, ensemble, owner, inflation, obs_block, obs_value, obs_std):
    p = Plan(grid, narrow, *ensemble.shape, obs_value.shape[0])
    dma = pltpu.SemaphoreType.DMA
    vmem, smem = pl.BlockSpec(memory_space=pltpu.VMEM), pl.BlockSpec(memory_space=pltpu.SMEM)
    anywhere = pl.BlockSpec(memory_space=pl.ANY)
    square = (p.m, p.m)
    scratch = [
        pltpu.VMEM((p.states // 128, p.ml, 128), BF16),
        pltpu.VMEM((p.narrow, p.ml, p.oshare), BF16),
        pltpu.VMEM((p.narrow, p.ml, p.oshare), BF16),
        pltpu.VMEM((p.m, p.oshare), BF16),
        pltpu.VMEM((2, p.peers, p.ra, 128), BF16),
        pltpu.VMEM((2, p.nz, p.tb, 128), BF16),
        pltpu.VMEM((p.peers, p.ra, 128), BF16),
        pltpu.VMEM((p.nz, p.tb, 128), BF16),
        pltpu.VMEM((p.peers, p.ra, 128), BF16),
        pltpu.VMEM((p.nz, p.tb, 128), BF16),
        pltpu.VMEM((p.peers, p.ra, 128), BF16),
        pltpu.VMEM((p.nz, p.tb, 128), BF16),
        pltpu.VMEM((p.nz, p.ra, 128), BF16),
        pltpu.VMEM((p.nx, p.tb, 128), BF16),
        pltpu.VMEM((p.ny, p.tb, 128), BF16),
        pltpu.VMEM((16, 128), F32),
        pltpu.VMEM((1, p.m), F32),
        pltpu.VMEM((2, p.half * 128, 128), BF16),
        pltpu.VMEM(square, BF16),
        pltpu.VMEM(square, BF16),
        pltpu.VMEM(square, BF16),
        pltpu.VMEM(square, F32),
        pltpu.VMEM(square, BF16),
        pltpu.VMEM(square, F32),
        pltpu.VMEM(square, BF16),
        pltpu.VMEM((p.narrow, p.ml, p.share), BF16),
        pltpu.VMEM((p.m, p.share), BF16),
        pltpu.VMEM(square, BF16),
        pltpu.VMEM((p.ny, 256, p.share), BF16),
        dma, dma((p.narrow,)), dma((p.narrow,)),
        dma((2,)), dma((2,)),
        dma((p.peers,)), dma((p.peers,)), dma((p.nz,)), dma((p.nz,)),
        dma((p.nz,)), dma((p.nz,)), dma((p.nx,)), dma((p.nx,)), dma((p.ny,)), dma((p.ny,)),
        dma((p.peers,)), dma((p.peers,)), dma((p.nz,)), dma((p.nz,)),
        dma((p.peers,)), dma((p.peers,)), dma((p.nz,)), dma((p.nz,)),
        dma((p.narrow, 2)), dma((p.narrow, 2)),
        dma, dma((p.ny, 2)), dma((p.narrow,)),
    ]
    return pl.pallas_call(
        functools.partial(kernel, p),
        out_shape=jax.ShapeDtypeStruct(ensemble.shape, BF16),
        in_specs=[smem, smem, smem, anywhere, vmem, vmem],
        out_specs=anywhere,
        scratch_shapes=scratch,
        compiler_params=pltpu.CompilerParams(
            collective_id=0, has_side_effects=True, vmem_limit_bytes=56 * 1024 * 1024
        ),
        name="etkf",
    )(owner, inflation, obs_block, ensemble, obs_value.reshape(-1, 128), obs_std.reshape(-1, 128))


def solution(mesh):
    wide, narrow = mesh.shape["wide"], mesh.shape["narrow"]
    grid = (4, wide // 4) if wide >= 16 else (2, wide // 2)
    return jax.shard_map(
        functools.partial(on_device, grid, narrow),
        mesh=mesh,
        in_specs=(P("narrow", "wide"), P("wide"), P(), P("wide"), P("wide"), P("wide")),
        out_specs=P("narrow", "wide"),
        check_vma=False,
    )
```

time: 109 us -> 94.2 us (0.86)
  Pallas kernels: 106 us -> 90.8 us
    pallas_call x1, Pallas kernels: 106 us -> 90.8 us  [on_device(): pl.pallas_call(functools.partial(kernel, p), out_shape=jax.ShapeDtypeStru...]
where the time goes in v2:
time: 94.2 us; the launch traced here: 93.9 us
  Pallas kernels  90.8 us (96%)
  local copies, waits for them, and re-layouts  3.1 us (3%)
    pallas_call x1, Pallas kernels, on_device(): pl.pallas_call(functools.partial(kernel, p), out_shape=jax.ShapeDtypeStru...  90.8 us
    unnamed x1, local copies, waits for them, and re-layouts  3.1 us

profile of v2, /device:TPU:1, one launch (start us, length us, event | category | flops | bytes accessed | tf_op | source)
XLA Modules:
  0.0 93.9 jit_solution(7006232698701482040)
XLA Ops:
  0.0 90.8 %etkf.1 = bf16[128,8192]{1,0:T(8,128)(2,1)} custom-call(s32[64]{0:T(128)} %owner.1, f32[256]{0:T(256)} %infl.1, s32[16]{0:T(128)} %oblk.1, bf16[128,8192]{1,0:T(8,128)(2,1)} %ens.1, f32[16,128]{1,0:T(8,128)} %bitcast.2, f32[16,128]{1,0:T(8,128)} %bitcast.3), custom_call_target="tpu_custom_call" | custom-call | tf_op jit(solution)/shard_map/etkf/pallas_call | solution.py:576
  90.8 3.1 %copy.8 = bf16[128,8192]{1,0:T(8,128)(2,1)} copy(bf16[128,8192]{1,0:T(8,128)(2,1)} %etkf.1) | data formatting | bytes 4194304

commit v3 on v2

--- a/solution.py
+++ b/solution.py
@@ -13,7 +13,7 @@
 F32 = jnp.float32
 BF16 = jnp.bfloat16
 NT = (((1,), (1,)), ((), ()))
-RAW_AT = ((None, None, 0, 0), (4, 4, 4, 4), (0, 1, 2, 4))
+RAW_AT = ((None, None, 0, 0), (4, 4, 4, 4), (0, 2, 1, 4))
 
 
 class Plan:
@@ -116,14 +116,12 @@
         cols = pl.ds(pl.multiple_of(b * 128, 128), 128)
         return pltpu.make_async_copy(ens.at[:, cols], ens_v.at[b], load_sem)
 
-    count = p.states // 128
-    lax.fori_loop(0, count, lambda b, carry: (load_block(b).start(), carry)[1], 0)
-
     barrier = pltpu.get_barrier_semaphore()
     greeted = 0
     for k in p.near:
         pl.semaphore_signal(barrier, inc=1, device_id=(w, near(k)), device_id_type=MESH)
         greeted += 1
+    lax.fori_loop(0, p.states // 128, lambda b, carry: (load_block(b).start(), carry)[1], 0)
     for t in range(1, p.nz):
         pl.semaphore_signal(barrier, inc=1, device_id=along_id(along(t)), device_id_type=MESH)
         greeted += 1
@@ -173,13 +171,13 @@
         return copy_to(ens.at[:, half_cols(frm, h)], half_slot(frm, h), raw_s.at[0, 0], raw_r.at[frm, h], (w, frm))
 
     def raw_start(when):
-        for k in p.near:
-            for h in range(2):
+        for h in range(2):
+            for k in p.near:
                 if RAW_AT[min(k[0], p.ny - k[0])][2 * k[1] + h] == when:
                     raw_copy(k, h).start()
                     pending.append(raw_copy(k, h))
 
-    own = pltpu.make_async_copy(ens.at[:, share_cols(n)], raw.at[n], own_sem)
+    own = pltpu.make_async_copy(ens.at[:, share_cols(n)], raw.at[n], own_sem.at[0])
     own.start()
     raw_start(0)
 
@@ -415,41 +413,41 @@
     def corner(s):
         return slice(0, (s + 1) * p.strip), slice(s * p.strip, (s + 1) * p.strip)
 
-    for s in range(strips):
+    for s in reversed(range(strips)):
         rows, cols = corner(s)
         unit = gram[rows, cols].astype(F32) * inv
         unit2 = mm(gram[rows, :], gram[:, cols]) * (inv * inv)
         put(prod, s, unit2)
         put(mix, s, 0.0625 * unit2 - 0.5625 * unit)
         est[rows, cols] = 1.6875 * unit2 - 2.4375 * unit
-    for s in range(strips):
+    for s in reversed(range(strips)):
         rows, cols = corner(s)
         new = est[rows, cols] + mm(prod[rows, :], mix[:, cols])
         est[rows, cols] = new
         put(estb, s, new)
-    for s in range(strips):
+    for s in reversed(range(strips)):
         rows, cols = corner(s)
         half = gram[rows, cols].astype(F32) * (2.25 * inv) + mm(gram[rows, :], estb[:, cols]) * inv
         more[rows, cols] = half
         put(prod, s, half)
-    for s in range(strips):
+    for s in reversed(range(strips)):
         rows, cols = corner(s)
         unit = 2.25 * more[rows, cols] + mm(prod[rows, :], estb[:, cols])
         more[rows, cols] = unit
         put(mix, s, unit)
-    for s in range(strips):
+    for s in reversed(range(strips)):
         rows, cols = corner(s)
         unit = more[rows, cols]
         unit2 = mm(mix[rows, :], mix[:, cols])
         put(prod, s, unit2)
         put(moreb, s, 0.0625 * unit2 - 0.5625 * unit)
         more[rows, cols] = 1.6875 * unit2 - 2.4375 * unit
-    for s in range(strips):
+    for s in reversed(range(strips)):
         rows, cols = corner(s)
         new = more[rows, cols] + mm(prod[rows, :], moreb[:, cols])
         put(mix, s, new)
         est[rows, cols] = 2.25 * (est[rows, cols] + new)
-    for s in range(strips):
+    for s in reversed(range(strips)):
         rows, cols = corner(s)
         new = est[rows, cols] + mm(estb[rows, :], mix[:, cols])
         row_ids = lax.broadcasted_iota(jnp.int32, new.shape, 0)
@@ -474,58 +472,80 @@
 
     lax.fori_loop(0, p.m // 128, transform_rows, 0)
 
-    for k in p.near:
-        raw_arrival(k, 0).wait_recv()
-        raw_arrival(k, 1).wait_recv()
-    own.wait()
-    state_mean = jnp.zeros((1, p.share), F32)
-    for k in range(p.narrow):
-        state_mean = state_mean + jnp.sum(raw[k].astype(F32), axis=0, keepdims=True)
-    state_mean = state_mean / p.m
-    factors = [
-        jnp.full((1, 128), infl[owner[n * (p.share // 128) + b]], F32) for b in range(p.share // 128)
-    ]
-    factors = jnp.concatenate(factors, axis=1)
-    for k in range(p.narrow):
-        anom[k * 128 : k * 128 + 128, :] = (factors * (raw[k].astype(F32) - state_mean)).astype(BF16)
-
-    def out_copy(dy, core):
+    per_half = p.share // 2
+
+    def out_copy(dy, core, h):
         there = lax.rem(y + dy, p.ny) * 2 + core
+        cols = pl.ds(h * per_half, per_half)
         return copy_to(
-            stage.at[dy, pl.ds(core * 128, 128), :], out.at[:, share_cols(n)], out_s.at[dy, core],
-            out_r.at[n], (w, there)
+            stage.at[dy, pl.ds(core * 128, 128), cols], out.at[:, half_cols(n, h)], out_s.at[dy, core, h], out_r.at[n, h], (w, there)
         )
 
-    def out_arrival(frm):
-        return copy_to(
-            stage.at[0, pl.ds(0, 128), :], out.at[:, share_cols(frm)], out_s.at[0, 0], out_r.at[frm], (w, frm)
-        )
-
-    def analyse(dy):
+    def out_arrival(k, h):
+        cols = pl.ds(h * per_half, per_half)
+        slot = out.at[:, half_cols(near(k), h)]
+        return copy_to(stage.at[0, pl.ds(0, 128), cols], slot, out_s.at[0, 0, h], out_r.at[near(k), h], (w, near(k)))
+
+    def analyse(dy, h, mean):
         rows = pl.ds(pl.multiple_of(lax.rem(y + dy, p.ny) * 256, 256), 256)
-        stage[dy] = (state_mean + mm(tmat[rows, :], anom[...])).astype(BF16)
+        cols = slice(h * per_half, (h + 1) * per_half)
+        stage[dy, :, cols] = (mean + mm(tmat[rows, :], anom[:, cols])).astype(BF16)
 
     order = sorted(range(1, p.ny), key=lambda d: -min(d, p.ny - d))
-    for dy in order:
-        analyse(dy)
-        for core in range(2):
-            out_copy(dy, core).start()
-    analyse(0)
-    to_sibling = copy_to(
-        stage.at[0, pl.ds(pl.multiple_of((1 - c) * 128, 128), 128), :], out.at[:, share_cols(n)], out_s.at[0, 0], out_r.at[n], sibling
-    )
-    to_sibling.start()
-    keep = pltpu.make_async_copy(
-        stage.at[0, pl.ds(pl.multiple_of(c * 128, 128), 128), :], out.at[:, share_cols(n)], own_sem
-    )
-    keep.start()
-
-    for k in p.near:
-        out_arrival(near(k)).wait_recv()
-    keep.wait()
-    pending.append(to_sibling)
-    pending += [out_copy(dy, core) for dy in order for core in range(2)]
+    means = []
+    for h in range(2):
+        for k in p.near:
+            raw_arrival(k, h).wait_recv()
+        if h == 0:
+            own.wait()
+        cols = slice(h * per_half, (h + 1) * per_half)
+        mean = jnp.zeros((1, per_half), F32)
+        for k in range(p.narrow):
+            mean = mean + jnp.sum(raw[k, :, cols].astype(F32), axis=0, keepdims=True)
+        mean = mean / p.m
+        means.append(mean)
+        first = n * (p.share // 128) + h * (per_half // 128)
+        factors = [jnp.full((1, 128), infl[owner[first + b]], F32) for b in range(per_half // 128)]
+        factors = jnp.concatenate(factors, axis=1)
+        for k in range(p.narrow):
+            anom[k * 128 : k * 128 + 128, cols] = (factors * (raw[k, :, cols].astype(F32) - mean)).astype(BF16)
+        for dy in order:
+            analyse(dy, h, mean)
+            for core in range(2):
+                out_copy(dy, core, h).start()
+                pending.append(out_copy(dy, core, h))
+    for h in range(2):
+        analyse(0, h, means[h])
+    rest = []
+    for h in range(2):
+        cols = pl.ds(h * per_half, per_half)
+        theirs = stage.at[0, pl.ds(pl.multiple_of((1 - c) * 128, 128), 128), cols]
+        mine = stage.at[0, pl.ds(pl.multiple_of(c * 128, 128), 128), cols]
+        to_sibling = copy_to(theirs, out.at[:, half_cols(n, h)], out_s.at[0, 0, h], out_r.at[n, h], sibling)
+        to_sibling.start()
+        pending.append(to_sibling)
+        keep = pltpu.make_async_copy(mine, out.at[:, half_cols(n, h)], own_sem.at[h])
+        keep.start()
+        rest.append(keep)
+    for h in range(2):
+        for k in p.near:
+            out_arrival(k, h).wait_recv()
+    for keep in rest:
+        keep.wait()
     finish(pending)
+
+
+def hand_on(parts, done, out, hold, in_sems, out_sems):
+    rows = [pl.ds(k * (done.shape[0] // parts), done.shape[0] // parts) for k in range(parts)]
+    reads = [pltpu.make_async_copy(done.at[r], hold.at[r], in_sems.at[k]) for k, r in enumerate(rows)]
+    writes = [pltpu.make_async_copy(hold.at[r], out.at[r], out_sems.at[k]) for k, r in enumerate(rows)]
+    for read in reads:
+        read.start()
+    for read, write in zip(reads, writes):
+        read.wait()
+        write.start()
+    for write in writes:
+        write.wait()
 
 
 def on_device(grid, narrow, ensemble, owner, inflation, obs_block, obs_value, obs_std):
@@ -571,9 +591,9 @@
         dma((p.peers,)), dma((p.peers,)), dma((p.nz,)), dma((p.nz,)),
         dma((p.peers,)), dma((p.peers,)), dma((p.nz,)), dma((p.nz,)),
         dma((p.narrow, 2)), dma((p.narrow, 2)),
-        dma, dma((p.ny, 2)), dma((p.narrow,)),
+        dma((2,)), dma((p.ny, 2, 2)), dma((p.narrow, 2)),
     ]
-    return pl.pallas_call(
+    done = pl.pallas_call(
         functools.partial(kernel, p),
         out_shape=jax.ShapeDtypeStruct(ensemble.shape, BF16),
         in_specs=[smem, smem, smem, anywhere, vmem, vmem],
@@ -584,6 +604,16 @@
         ),
         name="etkf",
     )(owner, inflation, obs_block, ensemble, obs_value.reshape(-1, 128), obs_std.reshape(-1, 128))
+    parts = p.ml // 16
+    return pl.pallas_call(
+        functools.partial(hand_on, parts),
+        out_shape=jax.ShapeDtypeStruct(ensemble.shape, BF16),
+        in_specs=[anywhere],
+        out_specs=anywhere,
+        scratch_shapes=[pltpu.VMEM(ensemble.shape, BF16), dma((parts,)), dma((parts,))],
+        compiler_params=pltpu.CompilerParams(vmem_limit_bytes=56 * 1024 * 1024),
+        name="hand_on",
+    )(done)
 
 
 def solution(mesh):

time: 94.2 us -> 91.7 us (0.973)
  local copies, waits for them, and re-layouts: 3.1 us -> 0 us
    unnamed x1 -> x0, local copies, waits for them, and re-layouts: 3.1 us -> none
    pallas_call x0 -> x1, Pallas kernels: none -> 2.39 us  [on_device(): pl.pallas_call(functools.partial(hand_on, parts), out_shape=jax.ShapeDtyp...]
    pallas_call x1, Pallas kernels: 90.8 us -> 88.9 us  [on_device(): pl.pallas_call(functools.partial(kernel, p), out_shape=jax.ShapeDtypeStru...]
where the time goes in v3:
time: 91.7 us; the launch traced here: 91.5 us
  Pallas kernels  91.3 us (100%)
    pallas_call x1, Pallas kernels, on_device(): pl.pallas_call(functools.partial(kernel, p), out_shape=jax.ShapeDtypeStru...  88.9 us
    pallas_call x1, Pallas kernels, on_device(): pl.pallas_call(functools.partial(hand_on, parts), out_shape=jax.ShapeDtyp...  2.39 us

profile of v3, /device:TPU:1, one launch (start us, length us, event | category | flops | bytes accessed | tf_op | source)
XLA Modules:
  0.0 91.5 jit_solution(1894940754937942207)
XLA Ops:
  0.0 88.9 %etkf.1.done = bf16[128,8192]{1,0:T(8,128)(2,1)} custom-call(s32[64]{0:T(128)} %owner.1, f32[256]{0:T(256)} %infl.1, s32[16]{0:T(128)} %oblk.1, bf16[128,8192]{1,0:T(8,128)(2,1)} %ens.1, f32[16,128]{1,0:T(8,128)} %bitcast.2, f32[16,128]{1,0:T(8,128)} %bitcast.3), custom_call_target="tpu_custom_call" | custom-call | tf_op jit(solution)/shard_map/etkf/pallas_call | solution.py:596
  88.9 2.4 %hand_on.1 = bf16[128,8192]{1,0:T(8,128)(2,1)} custom-call(bf16[128,8192]{1,0:T(8,128)(2,1)} %etkf.1.done), custom_call_target="tpu_custom_call" | custom-call | tf_op jit(solution)/shard_map/hand_on/pallas_call | solution.py:608

commit v4 on v3

--- a/solution.py
+++ b/solution.py
@@ -493,6 +493,7 @@
 
     order = sorted(range(1, p.ny), key=lambda d: -min(d, p.ny - d))
     means = []
+    early, pending = pending, []
     for h in range(2):
         for k in p.near:
             raw_arrival(k, h).wait_recv()
@@ -527,11 +528,12 @@
         keep = pltpu.make_async_copy(mine, out.at[:, half_cols(n, h)], own_sem.at[h])
         keep.start()
         rest.append(keep)
-    for h in range(2):
-        for k in p.near:
-            out_arrival(k, h).wait_recv()
+    finish(early)
     for keep in rest:
         keep.wait()
+    for h in range(2):
+        for k in reversed(p.near):
+            out_arrival(k, h).wait_recv()
     finish(pending)
 
 

time: 91.7 us -> 91.2 us (level)
  no operation moved by 1% of the time
where the time goes in v4:
time: 91.2 us; the launch traced here: 90.9 us
  Pallas kernels  90.7 us (99%)
    pallas_call x1, Pallas kernels, on_device(): pl.pallas_call(functools.partial(kernel, p), out_shape=jax.ShapeDtypeStru...  88.4 us
    pallas_call x1, Pallas kernels, on_device(): pl.pallas_call(functools.partial(hand_on, parts), out_shape=jax.ShapeDtyp...  2.39 us

profile of v4, /device:TPU:1, one launch (start us, length us, event | category | flops | bytes accessed | tf_op | source)
XLA Modules:
  0.0 90.9 jit_solution(8919822049455839392)
XLA Ops:
  0.0 88.4 %etkf.1.done = bf16[128,8192]{1,0:T(8,128)(2,1)} custom-call(s32[64]{0:T(128)} %owner.1, f32[256]{0:T(256)} %infl.1, s32[16]{0:T(128)} %oblk.1, bf16[128,8192]{1,0:T(8,128)(2,1)} %ens.1, f32[16,128]{1,0:T(8,128)} %bitcast.2, f32[16,128]{1,0:T(8,128)} %bitcast.3), custom_call_target="tpu_custom_call" | custom-call | tf_op jit(solution)/shard_map/etkf/pallas_call | solution.py:598
  88.4 2.4 %hand_on.1 = bf16[128,8192]{1,0:T(8,128)(2,1)} custom-call(bf16[128,8192]{1,0:T(8,128)(2,1)} %etkf.1.done), custom_call_target="tpu_custom_call" | custom-call | tf_op jit(solution)/shard_map/hand_on/pallas_call | solution.py:610

commit v5 on v4

--- a/solution.py
+++ b/solution.py
@@ -465,12 +465,11 @@
     shift = lax.fori_loop(0, p.m // 128, shift_rows, jnp.zeros((1, p.m), F32))
     shift = shift * (inv / root_scale)
 
-    def transform_rows(s, carry):
-        rows = pl.ds(pl.multiple_of(s * 128, 128), 128)
-        tmat[rows, :] = (est[rows, :] * inv_root + shift).astype(BF16)
-        return carry
-
-    lax.fori_loop(0, p.m // 128, transform_rows, 0)
+    def chip_rows(dy):
+        return pl.ds(pl.multiple_of(lax.rem(y + dy, p.ny) * 256, 256), 256)
+
+    def transform(dy):
+        tmat[chip_rows(dy), :] = (est[chip_rows(dy), :] * inv_root + shift).astype(BF16)
 
     per_half = p.share // 2
 
@@ -487,7 +486,9 @@
         return copy_to(stage.at[0, pl.ds(0, 128), cols], slot, out_s.at[0, 0, h], out_r.at[near(k), h], (w, near(k)))
 
     def analyse(dy, h, mean):
-        rows = pl.ds(pl.multiple_of(lax.rem(y + dy, p.ny) * 256, 256), 256)
+        rows = chip_rows(dy)
+        if h == 0:
+            transform(dy)
         cols = slice(h * per_half, (h + 1) * per_half)
         stage[dy, :, cols] = (mean + mm(tmat[rows, :], anom[:, cols])).astype(BF16)
 

time: 91.2 us -> 90.8 us (level)
  no operation moved by 1% of the time
where the time goes in v5:
time: 90.8 us; the launch traced here: 90.6 us
  Pallas kernels  90.4 us (100%)
    pallas_call x1, Pallas kernels, on_device(): pl.pallas_call(functools.partial(kernel, p), out_shape=jax.ShapeDtypeStru...  88 us
    pallas_call x1, Pallas kernels, on_device(): pl.pallas_call(functools.partial(hand_on, parts), out_shape=jax.ShapeDtyp...  2.39 us

profile of v5, /device:TPU:1, one launch (start us, length us, event | category | flops | bytes accessed | tf_op | source)
XLA Modules:
  0.0 90.6 jit_solution(14242300057286148458)
XLA Ops:
  0.0 88.0 %etkf.1.done = bf16[128,8192]{1,0:T(8,128)(2,1)} custom-call(s32[64]{0:T(128)} %owner.1, f32[256]{0:T(256)} %infl.1, s32[16]{0:T(128)} %oblk.1, bf16[128,8192]{1,0:T(8,128)(2,1)} %ens.1, f32[16,128]{1,0:T(8,128)} %bitcast.2, f32[16,128]{1,0:T(8,128)} %bitcast.3), custom_call_target="tpu_custom_call" | custom-call | tf_op jit(solution)/shard_map/etkf/pallas_call | solution.py:599
  88.0 2.4 %hand_on.1 = bf16[128,8192]{1,0:T(8,128)(2,1)} custom-call(bf16[128,8192]{1,0:T(8,128)(2,1)} %etkf.1.done), custom_call_target="tpu_custom_call" | custom-call | tf_op jit(solution)/shard_map/hand_on/pallas_call | solution.py:611
